TPU v7x, 512 devices: a whole 4x8x8 slice. The times are simulated.
512 devices in a mesh: rec: 16 (over z, core), frame: 32 (over x, y).
Axes of the slice: x: 4, y: 8, z: 8, core: 2. Of those that a mesh axis runs over, the one named last changes fastest.
Arguments:
- frames: bfloat16 [16, 49152, 256], P('rec', 'frame'), may hold values from -10 to 10
- texts: bfloat16 [32, 224, 256], P('rec', 'frame'), may hold values from -100 to 100
- pair_rec: int32 [32, 1], replicated, may hold values from 0 to 15, as said below
- pair_text: int32 [32], replicated, may hold values from 0 to 31, as said below
- pair_label: int32 [32], replicated, may hold values 0 or 1
Outputs:
- loss: float32 [], replicated
- grad_frames: bfloat16 [16, 49152, 256], P('rec', 'frame')
- grad_texts: bfloat16 [32, 224, 256], P('rec', 'frame')
Inputs may be any that keep to these rules, and one draw needn't show every extreme that they name: `pair_rec`: no recording is named by more than 6 pairs, some recording by exactly 6, and every recording by at least one. A pair's text is held by the index of rec one after, one before, or 8 after its recording (counted round): pair_text // 2 = (pair_rec + k) mod 16 with k one of 1, 15, 8.
All inputs are finite; a program needn't handle non-finite values.
Results may differ from a plain program's by a relative error of at most 0.0085.
Values may be sent and summed in bfloat16 or wider, within the bound.
A program may use at most 64 MiB of HBM per device.

v0:
```python
import jax
import jax.numpy as jnp
from jax import lax
from jax.sharding import PartitionSpec as P

MOST = 6
EPS = 1e-06
TEMP = 10.0
BIAS = -1.0
LOSS_SCALE = 2048.0


def slot_tables(pair_rec, pair_text, pair_label, here, most):
    record = pair_rec[:, 0]
    count = record.shape[0]
    order = jnp.arange(count, dtype=jnp.int32)
    same = (record[:, None] == record[None, :]).astype(jnp.int32)
    earlier = (order[None, :] < order[:, None]).astype(jnp.int32)
    rank = jnp.sum(same * earlier, axis=1)
    places = jnp.arange(most, dtype=jnp.int32)
    chosen = ((record[None, :] == here) & (rank[None, :] == places[:, None])).astype(jnp.int32)
    valid = jnp.sum(chosen, axis=1)
    slot_text = jnp.sum(chosen * pair_text[None, :], axis=1)
    sign = jnp.sum(chosen * (2 * pair_label[None, :] - 1), axis=1)
    return (valid, slot_text, sign)


def pair_terms(score, valid, sign, tokens):
    margin = -sign * (TEMP * score + BIAS)
    loss_part = valid * jax.nn.softplus(margin)
    grad_cos = -LOSS_SCALE * TEMP * valid * sign * jax.nn.sigmoid(margin) / tokens
    return (loss_part, grad_cos)


def body(frames, texts, pair_rec, pair_text, pair_label):
    here = lax.axis_index("rec")
    part = lax.axis_index("frame")
    owned, width_rows, width = texts.shape
    tokens = width_rows * lax.axis_size("frame")
    n_text = owned * lax.axis_size("rec")
    valid, slot_text, sign = slot_tables(pair_rec, pair_text, pair_label, here, MOST)
    valid_f = valid.astype(jnp.float32)
    sign_f = sign.astype(jnp.float32)
    picks = (
        (slot_text[:, None] == jnp.arange(n_text, dtype=jnp.int32)[None, :]) & (valid[:, None] > 0)
    ).astype(jnp.bfloat16)
    whole = lax.all_gather(texts, "frame", axis=1, tiled=True)
    query_vectors = jnp.einsum(
        "jc,cgx->jgx",
        picks,
        lax.all_gather(whole, "rec", axis=0, tiled=True),
        preferred_element_type=jnp.float32,
    ).astype(jnp.bfloat16)
    upstream_signal = frames[0]
    logit_scale = width ** (-0.5)
    pair_scores = (
        jnp.einsum(
            "ype,je->ypj", query_vectors, upstream_signal, preferred_element_type=jnp.float32
        )
        * logit_scale
    )
    local_max = jnp.max(pair_scores, axis=2)
    row_max = lax.pmax(local_max, "frame")
    expo = jnp.exp(pair_scores - row_max[..., None])
    batch_weights = expo.astype(jnp.bfloat16)
    value_partial = jnp.einsum(
        "pqx,xh->pqh", batch_weights, upstream_signal, preferred_element_type=jnp.float32
    )
    query_f = query_vectors.astype(jnp.float32)
    q_norm = lax.rsqrt(jnp.sum(query_f * query_f, axis=2) + EPS)
    q_unit = query_f * q_norm[..., None]
    context = lax.psum(value_partial, "frame")
    c_norm = lax.rsqrt(jnp.sum(context * context, axis=2) + EPS)
    c_unit = context * c_norm[..., None]
    cos = jnp.sum(q_unit * c_unit, axis=2)
    score = jnp.mean(cos, axis=1)
    loss_part, grad_cos = pair_terms(score, valid_f, sign_f, tokens)
    weight = grad_cos[:, None, None]
    d_context = weight * (q_unit - cos[..., None] * c_unit) * c_norm[..., None]
    direct = weight * (c_unit - cos[..., None] * q_unit) * q_norm[..., None]
    direct_own = lax.dynamic_slice_in_dim(direct, part * width_rows, width_rows, 1)
    context_batch_gradient = d_context.astype(jnp.bfloat16)
    weight_gradient = jnp.einsum(
        "ype,je->ypj", context_batch_gradient, upstream_signal, preferred_element_type=jnp.float32
    )
    score_gradient = (expo * weight_gradient * logit_scale).astype(jnp.bfloat16)
    d_query = lax.psum_scatter(
        jnp.einsum(
            "slf,fd->lsd", score_gradient, upstream_signal, preferred_element_type=jnp.float32
        ),
        "frame",
        scatter_dimension=0,
        tiled=True,
    )
    d_query = d_query + jnp.transpose(direct_own, (1, 0, 2))
    text_term = jnp.einsum(
        "st,lsd->tld", picks.astype(jnp.float32), d_query, precision=lax.Precision.HIGHEST
    )
    grad_texts = lax.psum_scatter(text_term, "rec", scatter_dimension=0, tiled=True).astype(
        jnp.bfloat16
    )
    frame_loss_piece = jnp.einsum(
        "cvm,cvz->mz", score_gradient, query_vectors, preferred_element_type=jnp.float32
    )
    frame_loss_piece = frame_loss_piece + jnp.einsum(
        "cvm,cvz->mz", batch_weights, context_batch_gradient, preferred_element_type=jnp.float32
    )
    grad_frames = frame_loss_piece.astype(jnp.bfloat16)[None]
    loss = lax.psum(jnp.sum(loss_part), "rec")
    return (loss, grad_frames, grad_texts)


def solution(mesh):
    return jax.shard_map(
        body,
        mesh=mesh,
        in_specs=(P("rec", "frame", None), P("rec", "frame", None), P(), P(), P()),
        out_specs=(P(), P("rec", "frame", None), P("rec", "frame", None)),
        check_vma=False,
    )
```

profile of v0, /device:TPU:16, one launch (start us, length us, event | category | flops | bytes accessed | tf_op | source)
XLA Modules:
  0.0 644.4 jit_solution(15901261809968272552)
XLA Ops:
  7.2 0.0 copy-start
  7.2 0.0 all-gather.2.cloned.1.call-start
  7.2 49.8 %all_gather.6 = bf16[2,224,256]{2,0,1:T(2,128)(2,1)S(1)} all-gather(bf16[2,7,256]{2,0,1:T(2,128)(2,1)} %param.6), channel_id=1, replica_groups=mesh['rec'=16,'frame'=32] {'frame'}, dimensions={1}, use_global_device_ids=true | all-gather | bytes 236544 | tf_op jit(solution)/shard_map/all_gather | solution.py:47
  57.0 0.7 copy.20
  57.7 0.0 all-gather.2.cloned.1.call-update
  57.8 0.0 all-reduce.5.cloned.1.call-start
  57.8 0.9 select_reduce_fusion
  58.7 0.7 broadcast_compare_fusion.1
  59.4 0.7 multiply_add_fusion
  60.1 1.3 select_reduce_fusion.2
  61.3 0.0 copy-start.9
  61.3 0.0 copy-start.4
  61.4 0.0 copy-start.8
  61.4 43.4 %all-gather.2.cloned.1.call-done = bf16[32,224,256]{2,1,0:T(8,128)(2,1)} async-done(((bf16[2,224,256]{2,1,0:T(8,128)(2,1)}), bf16[32,224,256]{2,1,0:T(8,128)(2,1)}) %all-gather.2.cloned.1.call-update) | async-done | bytes 3670032 | tf_op jit(solution)/shard_map/all_gather | solution.py:51
  104.7 0.0 copy-done.9
  104.7 4.3 fusion.6
  109.0 0.0 copy-done.4
  109.0 0.0 copy-done.8
  109.0 0.0 copy-done
  109.0 4.4 multiply_reduce_fusion
  113.4 71.4 %pmax.7 = f32[6,224]{1,0:T(8,128)S(1)} all-reduce(f32[6,224]{1,0:T(8,128)S(1)} %get-tuple-element.17), channel_id=1, replica_groups=mesh['rec'=16,'frame'=32] {'frame'}, use_global_device_ids=true, to_apply=%region_6.0 | all-reduce | flops 1344 | bytes 10752 | tf_op jit(solution)/shard_map/pmax | solution.py:63
  184.8 4.9 fusion.13
  189.7 2.1 copy.23
  191.7 0.0 all-reduce.5.cloned.1.call-update
  191.8 0.2 reduce-scatter.3.cloned.1.call-start
  192.0 0.7 add_rsqrt_fusion.1
  192.6 157.1 %all-reduce.5.cloned.1.call-done = f32[6,224,256]{2,0,1:T(8,128)} async-done(((f32[6,224,256]{2,0,1:T(8,128)}), f32[6,224,256]{2,0,1:T(8,128)}) %all-reduce.5.cloned.1.call-update) | async-done | bytes 1376272 | tf_op jit(solution)/shard_map/psum | solution.py:72
  349.7 0.0 copy-start.1
  349.7 1.9 multiply_reduce_fusion.1
  351.6 2.4 multiply_reduce_fusion.2
  354.0 0.0 copy-start.3
  354.0 1.4 fusion.44
  355.4 0.0 copy-start.6
  355.4 0.0 copy-done.1
  355.4 1.8 convert_multiply_fusion
  357.2 0.0 copy-done.3
  357.2 0.0 copy-start.2
  357.2 4.9 multiply_convert_fusion
  362.2 0.0 copy-done.6
  362.2 0.0 copy-done.2
  362.2 0.0 copy-start.10
  362.2 1.3 fusion.10
  363.5 0.7 copy-done.10
  364.2 2.1 copy.47
  366.2 0.0 reduce-scatter.3.cloned.1.call-update
  366.2 1.3 dynamic-slice
  368.2 0.7 constant_dynamic-slice_fusion
  368.9 0.7 constant_dynamic-slice_fusion.1
  369.6 0.0 copy-start.11
  369.6 5.7 convolution_bitcast_fusion
  375.2 0.0 copy-done.11
  375.3 0.0 copy-start.5
  375.3 0.0 copy-start.7
  375.3 2.3 fusion.5
  377.6 209.2 %reduce-scatter.3.cloned.1.call-done = f32[7,6,256]{2,1,0:T(8,128)} async-done(((f32[224,6,256]{2,1,0:T(8,128)}), f32[7,6,256]{2,1,0:T(8,128)}) %reduce-scatter.3.cloned.1.call-update) | async-done | bytes 43024 | tf_op jit(solution)/shard_map/reduce_scatter | solution.py:87
  586.9 0.0 copy-done.5
  586.9 0.0 copy-done.7
  586.9 1.3 fusion.27
  588.2 49.1 %all-reduce.6 = (f32[]{:T(128)}, bf16[32,7,256]{2,0,1:T(8,128)(2,1)S(1)}) all-reduce(f32[]{:T(128)} %get-tuple-element.14, f32[32,7,256]{2,0,1:T(8,128)S(1)} %fusion.27), channel_id=1, replica_groups=mesh['rec'=16,'frame'=32] {'rec'}, use_global_device_ids=true, to_apply=%region_11.12 | all-reduce | flops 57345 | bytes 344072 | tf_op jit(solution)/shard_map/psum | solution.py:109
  637.3 0.6 dynamic-slice_convert_fusion
  (2 shorter events, 0.0 us)
Async XLA Ops:
  7.2 101.8 %copy-start = (bf16[1,1536,256]{2,1,0:T(8,128)(2,1)S(1)}, bf16[1,1536,256]{2,1,0:T(8,128)(2,1)}, u32[]{:S(2)}) copy-start(bf16[1,1536,256]{2,1,0:T(8,128)(2,1)} %param.5) | copy-start | bytes 2359300
  7.2 97.5 %all-gather.2.cloned.1.call-start = ((), (), s32[]{:S(2)}) async-start(), calls=%async_computation.1 | async-start | bytes 3899392 | tf_op jit(solution)/shard_map/all_gather | solution.py:51
  57.8 291.9 %all-reduce.5.cloned.1.call-start = ((), (), s32[]{:S(2)}) async-start(), calls=%async_computation.2 | async-start | bytes 3670016 | tf_op jit(solution)/shard_map/psum | solution.py:72
  61.3 43.4 %copy-start.9 = (s32[6]{0:T(128)}, s32[6]{0:T(128)S(1)}, u32[]{:S(2)}) copy-start(s32[6]{0:T(128)S(1)} %get-tuple-element.7) | copy-start | bytes 76
  61.3 47.6 %copy-start.4 = (s32[6]{0:T(128)}, s32[6]{0:T(128)S(1)}, u32[]{:S(2)}) copy-start(s32[6]{0:T(128)S(1)} %get-tuple-element.6) | copy-start | bytes 76
  61.4 47.6 %copy-start.8 = (pred[6]{0:T(512)(128)(4,1)}, pred[6]{0:T(512)(128)(4,1)S(1)}, u32[]{:S(2)}) copy-start(pred[6]{0:T(512)(128)(4,1)S(1)} %broadcast_compare_fusion) | copy-start | bytes 22
  191.8 395.1 %reduce-scatter.3.cloned.1.call-start = ((), (), s32[]{:S(2)}) async-start(), calls=%async_computation.3 | async-start | bytes 1892352 | tf_op jit(solution)/shard_map/reduce_scatter | solution.py:87
  349.7 5.7 copy-start.1
  354.0 3.2 copy-start.3
  355.4 6.8 %copy-start.6 = (f32[6]{0:T(128)}, f32[6]{0:T(128)S(1)}, u32[]{:S(2)}) copy-start(f32[6]{0:T(128)S(1)} %get-tuple-element.13) | copy-start | bytes 76
  357.2 5.0 copy-start.2
  362.2 2.0 copy-start.10
  369.6 5.7 copy-start.11
  375.3 211.6 %copy-start.5 = (s32[6]{0:T(128)S(1)}, s32[6]{0:T(128)}, u32[]{:S(2)}) copy-start(s32[6]{0:T(128)} %copy-done.4) | copy-start | bytes 76
  375.3 211.6 %copy-start.7 = (f32[6]{0:T(128)S(1)}, f32[6]{0:T(128)}, u32[]{:S(2)}) copy-start(f32[6]{0:T(128)} %copy-done.6) | copy-start | bytes 76
Sparse Core Ops, SparseCore 0:
  57.9 46.7 all-gather.1
  191.9 157.7 all-reduce.4
  366.4 220.4 reduce-scatter.2
where the time goes:
time: 645 us; the launch traced here: 644 us
  waiting for transfers between devices  410 us (64%)
  blocking collectives  170 us (26%)
  matrix products  29 us (4%)
  between operations  14.6 us (2%)
  other arithmetic  11.7 us (2%)
  local copies, waits for them, and re-layouts  8.88 us (1%)
    reduce_scatter x1, waiting for transfers between devices, body(): lax.psum_scatter(jnp.einsum('slf,fd->lsd', score_gradient, upstream_signa...  209 us
    psum x1, waiting for transfers between devices, body(): context = lax.psum(value_partial, 'frame')  157 us
    pmax x1, blocking collectives, body(): row_max = lax.pmax(local_max, 'frame')  71.4 us
    all_gather x1, blocking collectives, body(): whole = lax.all_gather(texts, 'frame', axis=1, tiled=True)  49.8 us
    psum x1, blocking collectives, body(): loss = lax.psum(jnp.sum(loss_part), 'rec')  49.1 us
    all_gather x1, waiting for transfers between devices, body(): lax.all_gather(whole, 'rec', axis=0, tiled=True)  43.4 us
  transfers between devices with their start and end apart: 3, of which 3 were waited for; matrix products, arithmetic and copies ran while one was open for 2% of the time, Pallas kernels for 0%

commit v1 on v0

--- a/solution.py
+++ b/solution.py
@@ -69,7 +69,7 @@
     query_f = query_vectors.astype(jnp.float32)
     q_norm = lax.rsqrt(jnp.sum(query_f * query_f, axis=2) + EPS)
     q_unit = query_f * q_norm[..., None]
-    context = lax.psum(value_partial, "frame")
+    context = lax.all_gather(value_partial, "frame").sum(axis=0)
     c_norm = lax.rsqrt(jnp.sum(context * context, axis=2) + EPS)
     c_unit = context * c_norm[..., None]
     cos = jnp.sum(q_unit * c_unit, axis=2)

time: 645 us -> 796 us (1.23)
  waiting for transfers between devices: 410 us -> 549 us
  other arithmetic: 11.7 us -> 25.3 us
    all_gather x0 -> x1, waiting for transfers between devices: none -> 294 us  [body(): context = lax.all_gather(value_partial, 'frame').sum(axis=0)]
    psum x1 -> x0, waiting for transfers between devices: 157 us -> none  [body(): context = lax.psum(value_partial, 'frame')]
    reduce_sum x0 -> x1, other arithmetic: none -> 16.2 us  [body(): context = lax.all_gather(value_partial, 'frame').sum(axis=0)]
where the time goes in v1:
time: 796 us; the launch traced here: 795 us
  waiting for transfers between devices  549 us (69%)
  blocking collectives  170 us (21%)
  matrix products  30 us (4%)
  other arithmetic  25.3 us (3%)
  between operations  14.6 us (2%)
    all_gather x1, waiting for transfers between devices, body(): context = lax.all_gather(value_partial, 'frame').sum(axis=0)  294 us
    reduce_scatter x1, waiting for transfers between devices, body(): lax.psum_scatter(jnp.einsum('slf,fd->lsd', score_gradient, upstream_signa...  211 us
    pmax x1, blocking collectives, body(): row_max = lax.pmax(local_max, 'frame')  71.4 us
    all_gather x1, blocking collectives, body(): whole = lax.all_gather(texts, 'frame', axis=1, tiled=True)  49.8 us
    psum x1, blocking collectives, body(): loss = lax.psum(jnp.sum(loss_part), 'rec')  49.1 us
    all_gather x1, waiting for transfers between devices, body(): lax.all_gather(whole, 'rec', axis=0, tiled=True)  43.8 us
    reduce_sum x1, other arithmetic, body(): context = lax.all_gather(value_partial, 'frame').sum(axis=0)  16.2 us
  transfers between devices with their start and end apart: 3, of which 3 were waited for; matrix products, arithmetic and copies ran while one was open for 2% of the time, Pallas kernels for 0%

profile of v1, /device:TPU:16, one launch (start us, length us, event | category | flops | bytes accessed | tf_op | source)
XLA Modules:
  0.0 795.1 jit_solution(5661618880199912505)
XLA Ops:
  7.2 0.0 copy-start
  7.2 0.0 all-gather.4.cloned.1.call-start
  7.2 49.8 %all_gather.12 = bf16[2,224,256]{2,0,1:T(2,128)(2,1)S(1)} all-gather(bf16[2,7,256]{2,0,1:T(2,128)(2,1)} %param.6), channel_id=1, replica_groups=mesh['rec'=16,'frame'=32] {'frame'}, dimensions={1}, use_global_device_ids=true | all-gather | bytes 236544 | tf_op jit(solution)/shard_map/all_gather | solution.py:47
  57.0 0.7 copy.49
  57.7 0.0 all-gather.4.cloned.1.call-update
  57.8 0.0 all-gather.6.cloned.1.call-start
  57.8 0.9 select_reduce_fusion
  58.7 0.7 multiply_add_fusion
  59.4 0.7 broadcast_compare_fusion.1
  60.1 0.8 select_reduce_fusion.2
  60.9 43.8 %all-gather.4.cloned.1.call-done = bf16[32,224,256]{2,1,0:T(8,128)(2,1)} async-done(((bf16[2,224,256]{2,1,0:T(8,128)(2,1)}), bf16[32,224,256]{2,1,0:T(8,128)(2,1)}) %all-gather.4.cloned.1.call-update) | async-done | bytes 3670032 | tf_op jit(solution)/shard_map/all_gather | solution.py:51
  104.7 4.3 fusion.6
  109.0 0.0 copy-done
  109.0 4.6 multiply_reduce_fusion
  113.5 71.4 %pmax.7 = f32[6,224]{1,0:T(8,128)S(1)} all-reduce(f32[6,224]{1,0:T(8,128)S(1)} %get-tuple-element.17), channel_id=1, replica_groups=mesh['rec'=16,'frame'=32] {'frame'}, use_global_device_ids=true, to_apply=%region_6.0 | all-reduce | flops 1344 | bytes 10752 | tf_op jit(solution)/shard_map/pmax | solution.py:63
  184.9 5.9 fusion.13
  190.8 0.0 all-gather.6.cloned.1.call-update
  190.8 0.2 reduce-scatter.3.cloned.1.call-start
  191.1 0.1 copy.51
  191.2 0.1 copy.52
  191.3 293.6 %all-gather.6.cloned.1.call-done = f32[192,224,256]{2,1,0:T(8,128)} async-done(((f32[6,224,256]{2,1,0:T(8,128)}), f32[192,224,256]{2,1,0:T(8,128)}) %all-gather.6.cloned.1.call-update) | async-done | bytes 44040208 | tf_op jit(solution)/shard_map/all_gather | solution.py:72
  485.0 16.2 %reduce_sum.95 = f32[6,224,256]{2,1,0:T(8,128)S(1)} reduce(f32[32,6,224,256]{3,2,1,0:T(8,128)} %bitcast.44, f32[]{:T(128)} %constant.14.clone.1), dimensions={0}, to_apply=%region_7.0 | reduce | flops 10665984 | bytes 45416452 | tf_op jit(solution)/shard_map/reduce_sum | solution.py:72
  501.2 0.3 multiply_reduce_fusion.1
  501.5 0.1 copy.54
  501.6 2.4 multiply_reduce_fusion.2
  504.0 0.6 fusion.44
  504.6 2.7 copy_multiply_fusion
  507.3 0.0 copy-start.1
  507.3 4.9 multiply_convert_fusion
  512.3 0.0 copy-done.1
  512.3 0.0 copy-start.3
  512.3 1.3 fusion.10
  513.6 0.7 copy-done.3
  514.2 0.0 copy-start.2
  514.2 2.1 copy.86
  516.4 0.0 reduce-scatter.3.cloned.1.call-update
  516.4 1.3 dynamic-slice
  518.4 0.0 copy-done.2
  518.4 0.0 copy-start.4
  518.4 5.5 convolution_bitcast_fusion
  523.9 0.0 copy-done.4
  523.9 2.4 fusion.5
  526.2 211.3 %reduce-scatter.3.cloned.1.call-done = f32[7,6,256]{2,1,0:T(8,128)} async-done(((f32[224,6,256]{2,1,0:T(8,128)}), f32[7,6,256]{2,1,0:T(8,128)}) %reduce-scatter.3.cloned.1.call-update) | async-done | bytes 43024 | tf_op jit(solution)/shard_map/reduce_scatter | solution.py:87
  737.5 1.3 fusion.27
  738.8 49.1 %all-reduce.3 = (f32[]{:T(128)}, bf16[32,7,256]{2,0,1:T(8,128)(2,1)S(1)}) all-reduce(f32[]{:T(128)} %get-tuple-element.14, f32[32,7,256]{2,0,1:T(8,128)S(1)} %fusion.27), channel_id=1, replica_groups=mesh['rec'=16,'frame'=32] {'rec'}, use_global_device_ids=true, to_apply=%region_11.12 | all-reduce | flops 57345 | bytes 344072 | tf_op jit(solution)/shard_map/psum | solution.py:109
  788.0 0.6 dynamic-slice_convert_fusion
  (4 shorter events, 0.0 us)
Async XLA Ops:
  7.2 101.8 %copy-start = (bf16[1,1536,256]{2,1,0:T(8,128)(2,1)S(1)}, bf16[1,1536,256]{2,1,0:T(8,128)(2,1)}, u32[]{:S(2)}) copy-start(bf16[1,1536,256]{2,1,0:T(8,128)(2,1)} %param.5) | copy-start | bytes 2359300
  7.2 97.5 %all-gather.4.cloned.1.call-start = ((), (), s32[]{:S(2)}) async-start(), calls=%async_computation.1 | async-start | bytes 3899392 | tf_op jit(solution)/shard_map/all_gather | solution.py:51
  57.8 427.2 %all-gather.6.cloned.1.call-start = ((), (), s32[]{:S(2)}) async-start(), calls=%async_computation.3 | async-start | bytes 45416448 | tf_op jit(solution)/shard_map/all_gather | solution.py:72
  190.8 546.7 %reduce-scatter.3.cloned.1.call-start = ((), (), s32[]{:S(2)}) async-start(), calls=%async_computation.2 | async-start | bytes 1892352 | tf_op jit(solution)/shard_map/reduce_scatter | solution.py:87
  507.3 5.0 copy-start.1
  512.3 1.9 copy-start.3
  514.2 4.1 copy-start.2
  518.4 5.5 copy-start.4
Sparse Core Ops, SparseCore 0:
  57.9 46.7 all-gather.3
  191.0 293.9 all-gather.5
  516.5 220.9 reduce-scatter.2
